TPU v7x, 32 devices: a whole 2x2x4 slice. The times are simulated.
32 devices in a mesh: seq: 2 (over x), dp: 16 (over z, y, core).
Axes of the slice: x: 2, y: 2, z: 4, core: 2. Of those that a mesh axis runs over, the one named last changes fastest.
Arguments:
- layer_in: bfloat16 [32, 768, 768], P('dp', 'seq'), may hold values from -6 to 6
- segment: int32 [32, 768], P('dp', 'seq'), may hold values from -1 to 32, as said below
- key_mask: int32 [32, 768], P('dp', 'seq'), may hold values from 0 to 1, as said below
- position: int32 [32, 768], P('dp', 'seq'), may hold values from 0 to 196, as said below
- layout_x: int32 [32, 768], P('dp', 'seq'), may hold values from 0 to 47
- layout_y: int32 [32, 768], P('dp', 'seq'), may hold values from 0 to 47
- qkv_weight: bfloat16 [768, 2304], replicated, may hold values from -0.21875 to 0.21875
- query_bias: bfloat16 [768], replicated, may hold values from -3 to 3
- value_bias: bfloat16 [768], replicated, may hold values from -3 to 3
- out_weight: bfloat16 [768, 768], replicated, may hold values from -0.875 to 0.875
- out_bias: bfloat16 [768], replicated, may hold values from -3 to 3
- attn_gain: bfloat16 [768], replicated, may hold values from 0.5 to 1.5
- attn_shift: bfloat16 [768], replicated, may hold values from -3 to 3
- up_weight: bfloat16 [768, 3072], replicated, may hold values from -0.21875 to 0.21875
- up_bias: bfloat16 [3072], replicated, may hold values from -3 to 3
- down_weight: bfloat16 [3072, 768], replicated, may hold values from -0.109375 to 0.109375
- down_bias: bfloat16 [768], replicated, may hold values from -3 to 3
- ffn_gain: bfloat16 [768], replicated, may hold values from 0.5 to 1.5
- ffn_shift: bfloat16 [768], replicated, may hold values from -3 to 3
- text_table: bfloat16 [33, 12], replicated, may hold values from -3 to 3
- horiz_table: bfloat16 [33, 12], replicated, may hold values from -3 to 3
- vert_table: bfloat16 [33, 12], replicated, may hold values from -3 to 3
- cotangent: bfloat16 [32, 768, 768], P('dp', 'seq'), may hold values from -6 to 6
Outputs:
- layer_out: bfloat16 [32, 768, 768], P('dp', 'seq')
- grad_input: float32 [32, 768, 768], P('dp', 'seq')
- grad_qkv: float32 [768, 2304], replicated
- grad_query_bias: float32 [768], replicated
- grad_value_bias: float32 [768], replicated
- grad_out_weight: float32 [768, 768], replicated
- grad_out_bias: float32 [768], replicated
- grad_attn_gain: float32 [768], replicated
- grad_attn_shift: float32 [768], replicated
- grad_up_weight: float32 [768, 3072], replicated
- grad_up_bias: float32 [3072], replicated
- grad_down_weight: float32 [3072, 768], replicated
- grad_down_bias: float32 [768], replicated
- grad_ffn_gain: float32 [768], replicated
- grad_ffn_shift: float32 [768], replicated
- grad_text_table: float32 [33, 12], replicated
- grad_horiz_table: float32 [33, 12], replicated
- grad_vert_table: float32 [33, 12], replicated
Inputs may be any that keep to these rules, and one draw needn't show every extreme that they name: `segment`: rows 0 to 511 of an item hold forms with consecutive positive numbers rising in row order, each form of at most 64 rows, the last used form of every item numbered 512 // 16; then unused text rows marked -1; at least 448 text rows are used. Rows 512 to 708 are image patches marked 0, the remaining rows are padding marked -1. `key_mask`: 1 exactly where segment is not -1. `position`: the row's index within its form on text rows, the patch index on image rows, 0 on unused rows.
All inputs are finite; a program needn't handle non-finite values.
Results may differ from a plain program's by a relative error of at most 0.014.
Values may be sent and summed in bfloat16 or wider, within the bound.
A program may use at most 320 MiB of HBM per device.

v0:
```python
import functools

import jax
import jax.numpy as jnp
from jax import lax
from jax.experimental import pallas as pl
from jax.experimental.pallas import tpu as pltpu
from jax.sharding import PartitionSpec as P

BF = jnp.bfloat16
F32 = jnp.float32
BIG = 1e30
LANES = 128
HEAD = 64
TEXT = 512
POS = 64
COORD = 48
Y0 = 64
GROUP0 = 112
MEMBER0 = 116
FLAG = 124
EVERY = 125
STRAY = 126
X_TABLE = 33
Y_TABLE = 66
NOTHING = 127


def dot_nt(a, b):
    return lax.dot_general(a, b, (((1,), (1,)), ((), ())), preferred_element_type=F32)


def dot_nn(a, b):
    return lax.dot_general(a, b, (((1,), (0,)), ((), ())), preferred_element_type=F32)


def looked_up(table_row, index):
    rows = index.shape[0]
    return jnp.take_along_axis(
        jnp.broadcast_to(table_row, (rows, LANES)), index, axis=1, mode="promise_in_bounds"
    )


def bucket(distance):
    return jnp.clip(distance, -16, 16) + 16


def between(lane, low, high):
    return (lane >= low) & (lane < high)


def columns_of(meta_ref):
    return tuple(meta_ref[:, field : field + 1] for field in range(5))


def marks(meta_ref):
    segment, key_mask, position, across, down = columns_of(meta_ref)
    rows = segment.shape[0]
    lane = lax.broadcasted_iota(jnp.int32, (rows, LANES), 1)
    row = lax.broadcasted_iota(jnp.int32, (rows, LANES), 0)
    even = between(lane, HEAD, HEAD + COORD) & (lane - HEAD == across)
    odd = (lane < COORD) & (lane == across)
    group = (segment - 1) >> 3
    member = (segment - 1) & 7
    named = segment > 0
    shared = (
        ((row < TEXT) & (lane < POS) & (lane == position))
        | (between(lane, Y0, Y0 + COORD) & (lane - Y0 == down))
        | (named & between(lane, GROUP0, MEMBER0) & (lane - GROUP0 == group))
        | (named & between(lane, MEMBER0, FLAG) & (lane - MEMBER0 == member))
        | ((lane == FLAG) & (key_mask <= 0))
        | (lane == EVERY)
        | ((lane == STRAY) & (segment < 0))
    )
    return tuple(jnp.where(m, 1.0, 0.0).astype(BF) for m in (even, odd, shared))


def square_lanes():
    shape = (LANES, LANES)
    return lax.broadcasted_iota(jnp.int32, shape, 0), lax.broadcasted_iota(jnp.int32, shape, 1)


def barred():
    row, lane = square_lanes()
    in_groups = between(lane, GROUP0, MEMBER0)
    shut = (
        (between(row, GROUP0, MEMBER0) & in_groups & (lane != row))
        | (between(row, MEMBER0, FLAG) & between(lane, MEMBER0, FLAG) & (lane != row))
        | ((row == EVERY) & (lane == FLAG))
        | ((row == STRAY) & in_groups)
    )
    return jnp.where(shut, -BIG, 0.0).astype(F32)


def table_index():
    row, lane = square_lanes()
    distance = bucket(row - lane)
    inside = lambda low, high: between(row, low, high) & between(lane, low, high)
    even = jnp.where(inside(HEAD, HEAD + COORD), distance + X_TABLE, NOTHING)
    odd = jnp.where(inside(0, COORD), distance + X_TABLE, NOTHING)
    shared = jnp.where(
        inside(0, POS), distance, jnp.where(inside(Y0, Y0 + COORD), distance + Y_TABLE, NOTHING)
    )
    return even, odd, shared


def image_query_index(meta_ref):
    position = meta_ref[TEXT:, 2:3]
    lane = lax.broadcasted_iota(jnp.int32, (position.shape[0], LANES), 1)
    return jnp.where(lane < POS, bucket(position - lane), NOTHING)


def prepare(meta_ref, mark_refs, bar_ref, index_refs, image_index_ref):
    for ref, value in zip(mark_refs, marks(meta_ref)):
        ref[...] = value
    bar_ref[...] = barred()
    for ref, value in zip(index_refs, table_index()):
        ref[...] = value
    image_index_ref[...] = image_query_index(meta_ref)


def own_lanes(parity, rows):
    lane = lax.broadcasted_iota(jnp.int32, (rows, LANES), 1)
    return (lane < HEAD) if parity == 0 else (lane >= HEAD)


def widened(parity, q, table_row, bias, bar_ref, index_refs, image_index_ref, mark_refs):
    rows = q.shape[0]
    shared = mark_refs[2][...]
    across = looked_up(table_row, index_refs[parity][...]).astype(BF)
    first = jnp.where(
        own_lanes(parity, rows), q.astype(F32) * 0.125, dot_nn(mark_refs[parity][...], across)
    )
    others = (looked_up(table_row, index_refs[2][...]) + bar_ref[...]).astype(BF)
    second = dot_nn(shared, others)
    on_images = looked_up(table_row, image_index_ref[...])
    second = jnp.concatenate([second[:TEXT], second[TEXT:] + on_images], axis=0)
    image_lane = lax.broadcasted_iota(jnp.int32, on_images.shape, 1)
    key_image = jnp.where(image_lane < POS, bias[:, :LANES].astype(BF), shared[TEXT:])
    return first.astype(BF), second.astype(BF), key_image


def joined(parity, first, second, key_image, k, marks_own, shared):
    rows = k.shape[0]
    lane = lax.broadcasted_iota(jnp.int32, (rows, LANES), 1)
    to_image = jnp.where(lane < POS, shared, second)
    key_first = jnp.where(own_lanes(parity, rows), k, marks_own)
    q_text = jnp.concatenate([first, second], axis=1)
    q_image = jnp.concatenate([first, to_image], axis=1)
    k_text = jnp.concatenate([key_first[:TEXT], shared[:TEXT]], axis=1)
    k_image = jnp.concatenate([key_first[TEXT:], key_image], axis=1)
    return q_text, q_image, k_text, k_image


def near(start, size):
    if start >= TEXT:
        return slice(0, TEXT)
    return slice(max(0, start - LANES), min(TEXT, start + size + LANES))


def image_bias(table_row, offsets):
    return jnp.concatenate(
        [looked_up(table_row, offsets[:, :LANES]), looked_up(table_row, offsets[:, LANES:])], axis=1
    )


def forward_kernel(
    meta_ref, rows_ref, table_ref, q_ref, k_ref, v_ref,
    mixed_ref, log_ref, first_ref, second_ref, key_image_ref, bias_ref,
    even_ref, odd_ref, shared_ref, bar_ref, index_even, index_odd, index_shared, image_index_ref,
):
    mark_refs = (even_ref, odd_ref, shared_ref)
    index_refs = (index_even, index_odd, index_shared)

    @pl.when(pl.program_id(0) == 0)
    def _():
        prepare(meta_ref, mark_refs, bar_ref, index_refs, image_index_ref)

    rows = q_ref.shape[0]
    images = rows - TEXT
    q, k, v = q_ref[...], k_ref[...], v_ref[...]
    offsets = bucket(rows_ref[2:3, TEXT:] - meta_ref[TEXT:, 2:3])
    tile = 256
    v_turned = transposed(v)
    heads = [None, None]

    def prepared(parity):
        table_row = table_ref[pl.ds(2 * pl.program_id(0) + parity, 1), :]
        bias = image_bias(table_row, offsets)
        first, second, key_image = widened(
            parity, q, table_row, bias, bar_ref, index_refs, image_index_ref, mark_refs
        )
        first_ref[parity] = first
        second_ref[parity] = second
        key_image_ref[parity] = key_image
        bias_ref[parity] = bias.astype(BF)
        wide = joined(
            parity, first, second, key_image, k, mark_refs[parity][...], shared_ref[...]
        )
        heads[parity] = wide + (bias,)

    def scored(parity, start):
        q_text, q_image, k_text, k_image, bias = heads[parity]
        here = slice(start, start + tile)
        on_image = dot_nt(k_image, q_image[here])
        if start >= TEXT:
            on_image = on_image + bias[:, start - TEXT : start - TEXT + tile]
        return dot_nt(k_text[near(start, tile)], q_text[here]), on_image

    spots = [(parity, start) for parity in range(2) for start in range(0, rows, tile)]
    outs = ([], [])
    prepared(0)
    following = scored(*spots[0])
    for index, (parity, start) in enumerate(spots):
        on_text, on_image = following
        if index == 1:
            prepared(1)
        if index + 1 < len(spots):
            following = scored(*spots[index + 1])
        top = jnp.maximum(
            jnp.max(on_text, axis=0, keepdims=True), jnp.max(on_image, axis=0, keepdims=True)
        )
        on_text = jnp.exp(on_text - top)
        on_image = jnp.exp(on_image - top)
        total = jnp.sum(on_text, axis=0, keepdims=True) + jnp.sum(on_image, axis=0, keepdims=True)
        own = slice(parity * HEAD, parity * HEAD + HEAD)
        out = dot_nn(v_turned[own, near(start, tile)], on_text.astype(BF)) + dot_nn(
            v_turned[own, TEXT:], on_image.astype(BF)
        )
        outs[parity].append(out * (1.0 / total))
        log_ref[0, parity : parity + 1, start : start + tile] = top + jnp.log(total)
    mixed_ref[...] = jnp.transpose(
        jnp.concatenate([jnp.concatenate(outs[parity], axis=1) for parity in range(2)], axis=0)
    )


def static_scratch(rows):
    square = (LANES, LANES)
    return [
        pltpu.VMEM((rows, LANES), BF),
        pltpu.VMEM((rows, LANES), BF),
        pltpu.VMEM((rows, LANES), BF),
        pltpu.VMEM(square, F32),
        pltpu.VMEM(square, jnp.int32),
        pltpu.VMEM(square, jnp.int32),
        pltpu.VMEM(square, jnp.int32),
        pltpu.VMEM((rows - TEXT, LANES), jnp.int32),
    ]


def attention_forward(meta_columns, meta_rows, table_rows, projected, width):
    rows = projected.shape[0]
    images = rows - TEXT
    pairs = width // LANES

    def block(part):
        return pl.BlockSpec((rows, LANES), lambda p: (0, part * pairs + p))

    whole = lambda shape: pl.BlockSpec(shape, lambda p: (0,) * len(shape))
    return pl.pallas_call(
        forward_kernel,
        grid=(pairs,),
        in_specs=[
            whole(meta_columns.shape),
            whole(meta_rows.shape),
            whole(table_rows.shape),
            block(0), block(1), block(2),
        ],
        out_specs=[
            pl.BlockSpec((rows, LANES), lambda p: (0, p)),
            pl.BlockSpec((1, 2, rows), lambda p: (p, 0, 0)),
            pl.BlockSpec((2, rows, LANES), lambda p: (p, 0, 0)),
            pl.BlockSpec((2, rows, LANES), lambda p: (p, 0, 0)),
            pl.BlockSpec((2, images, LANES), lambda p: (p, 0, 0)),
            pl.BlockSpec((2, images, images), lambda p: (p, 0, 0)),
        ],
        out_shape=[
            jax.ShapeDtypeStruct((rows, width), F32),
            jax.ShapeDtypeStruct((pairs, 2, rows), F32),
            jax.ShapeDtypeStruct((2 * pairs, rows, LANES), BF),
            jax.ShapeDtypeStruct((2 * pairs, rows, LANES), BF),
            jax.ShapeDtypeStruct((2 * pairs, images, LANES), BF),
            jax.ShapeDtypeStruct((2 * pairs, images, images), BF),
        ],
        scratch_shapes=static_scratch(rows),
        compiler_params=pltpu.CompilerParams(vmem_limit_bytes=60 * 1024 * 1024),
        name="attention_forward",
    )(meta_columns, meta_rows, table_rows, projected, projected, projected)


def skewed(block):
    size = block.shape[0]
    lane = lax.broadcasted_iota(jnp.int32, (size, LANES), 1)
    row = lax.broadcasted_iota(jnp.int32, (size, LANES), 0)
    turned = jnp.take_along_axis(
        block, (lane + row) & (LANES - 1), axis=1, mode="promise_in_bounds"
    )
    straight = lane + row < LANES
    above = jnp.sum(jnp.where(straight, turned, 0.0), axis=0, keepdims=True)
    below = jnp.sum(jnp.where(straight, 0.0, turned), axis=0, keepdims=True)
    return above, below


def transposed(array):
    return jnp.transpose(array.astype(F32)).astype(array.dtype)


def static_prepare(meta_ref, static):
    for ref, turned, value in zip(static[:3], static[3:], marks(meta_ref)):
        ref[...] = value
        turned[...] = transposed(value)


def head_back(
    parity, pair, rows_ref, wide_refs, k_ref, v_ref, mixed_ref, grad_ref, log_ref, static, diag_ref,
):
    mark_refs, turned_refs = static[:3], static[3:]
    first_ref, second_ref, key_image_ref, bias_ref = wide_refs
    head = 2 * pair + parity
    shared_t = turned_refs[2]
    rows = k_ref.shape[1]
    images = rows - TEXT
    tile = 256
    k, v, grad = k_ref[pair], v_ref[pair], grad_ref[pair]
    products = grad.astype(F32) * mixed_ref[pair]
    k_turned = transposed(k)
    is_image = rows_ref[1:2, TEXT:] > 0
    own = own_lanes(parity, rows)
    log_row = log_ref[pair, parity : parity + 1, :]
    first, shared = first_ref[head], mark_refs[2][...]
    q_text, q_image, k_text, k_image = joined(
        parity, first, second_ref[head], key_image_ref[head], k, mark_refs[parity][...], shared
    )
    bias = bias_ref[head].astype(F32)
    ones = jnp.where(own_lanes(parity, 8), 1.0, 0.0).astype(BF)
    delta = jnp.zeros((8, rows), F32)
    rest = products
    for _ in range(3):
        piece = rest.astype(BF)
        delta = delta + dot_nt(ones, piece)
        rest = rest - piece.astype(F32)
    delta = delta[0:1]
    v_own = jnp.where(own, v, jnp.zeros_like(v))
    q_marked = jnp.concatenate(
        [jnp.where(own, first, mark_refs[parity][...]), shared], axis=1
    )
    dq_text = jnp.zeros((HEAD, TEXT), F32)
    dq_image = jnp.zeros((HEAD, images), F32)
    dks = []
    dvs = []
    first_sum = jnp.zeros((LANES, LANES), F32)
    second_sum = jnp.zeros((LANES, LANES), F32)
    text_image = jnp.zeros((LANES, images), F32)

    def met(start, array, axis=0):
        text = near(start, tile)
        if axis == 0:
            return jnp.concatenate([array[text], array[TEXT:]], axis=0)
        return jnp.concatenate([array[:, text], array[:, TEXT:]], axis=1)

    def scored(start):
        here = slice(start, start + tile)
        if start < TEXT:
            scores = dot_nt(k_text[here], met(start, q_text))
        else:
            scores = dot_nt(k_image[start - TEXT : start - TEXT + tile], q_image)
            scores = jnp.concatenate([scores[:, :TEXT], scores[:, TEXT:] + bias], axis=1)
        return scores, dot_nt(v_own[here], met(start, grad))

    following = scored(0)
    for start in range(0, rows, tile):
        here = slice(start, start + tile)
        scores, prob_grad = following
        if start + tile < rows:
            following = scored(start + tile)
        soft = jnp.exp(scores - met(start, log_row, 1))
        score_grad = soft * (prob_grad - met(start, delta, 1))
        low = score_grad.astype(BF)
        dvs.append(dot_nn(soft.astype(BF), met(start, grad)))
        wide = dot_nn(low, met(start, q_marked))
        dks.append(wide[:, :LANES])
        part = dot_nn(k_turned[parity * HEAD : parity * HEAD + HEAD, here], low)
        text = near(start, tile)
        count = text.stop - text.start
        before = [jnp.zeros((HEAD, text.start), F32)] if text.start > 0 else []
        after = [jnp.zeros((HEAD, TEXT - text.stop), F32)] if text.stop < TEXT else []
        dq_text = dq_text + jnp.concatenate(before + [part[:, :count]] + after, axis=1)
        dq_image = dq_image + part[:, count:]
        rounded = wide.astype(BF)
        first_sum = first_sum + dot_nn(turned_refs[parity][:, here], rounded[:, :LANES])
        second_sum = second_sum + dot_nn(shared_t[:, here], rounded[:, LANES:])
        if start < TEXT:
            text_image = text_image + dot_nn(shared_t[:, here], low[:, count:])
        else:
            by_position = wide[:, LANES:]
            on_image = score_grad[:, TEXT:]
    dq = jnp.concatenate([dq_text, dq_image], axis=1)
    small = lax.broadcasted_iota(jnp.int32, (LANES, LANES), 1)
    small_row = lax.broadcasted_iota(jnp.int32, (LANES, LANES), 0)
    x0 = HEAD if parity == 0 else 0
    x_block = jnp.where(
        between(small, x0, x0 + COORD) & between(small_row, x0, x0 + COORD), first_sum, 0.0
    )
    y_block = jnp.where(
        between(small, Y0, Y0 + COORD) & between(small_row, Y0, Y0 + COORD), second_sum, 0.0
    )
    p_block = jnp.where((small < POS) & (small_row < POS), second_sum, 0.0)
    wide_lane = lax.broadcasted_iota(jnp.int32, (images, images), 1)
    outside = jnp.sum(jnp.where(is_image, 0.0, on_image), axis=1, keepdims=True)
    pairs = jnp.where(is_image, on_image, 0.0) + jnp.where(wide_lane == 0, outside, 0.0)
    outside_text = jnp.sum(jnp.where(is_image, 0.0, text_image), axis=1, keepdims=True)
    text_lane = lax.broadcasted_iota(jnp.int32, (LANES, images), 1)
    text_row = lax.broadcasted_iota(jnp.int32, (LANES, images), 0)
    text_image = jnp.where(is_image, text_image, 0.0) + jnp.where(
        text_lane == 0, outside_text, 0.0
    )
    text_image = jnp.where(text_row < POS, text_image, 0.0)
    first_lane = lax.broadcasted_iota(jnp.int32, (images, LANES), 1)
    left = pairs[:, :LANES] + jnp.where(first_lane < POS, by_position, 0.0)
    right = pairs[:, LANES:]
    a00, b00 = skewed(left[:LANES] + text_image[:, :LANES] + p_block)
    a01, b01 = skewed(right[:LANES] + text_image[:, LANES:])
    a10, b10 = skewed(left[LANES:])
    a11, b11 = skewed(right[LANES:])
    ax, bx = skewed(x_block)
    ay, by = skewed(y_block)
    diag_ref[head] = jnp.concatenate(
        [b10, b00 + b11 + a10, a00 + a11 + b01, a01, bx, ax, by, ay], axis=0
    )
    return dq * 0.125, jnp.concatenate(dks, axis=0), jnp.concatenate(dvs, axis=0)


MESH = pl.DeviceIdType.MESH
VMEM = pl.BlockSpec(memory_space=pltpu.VMEM)
HBM = pl.BlockSpec(memory_space=pltpu.HBM)
MIB = 1024 * 1024


def remote(src, dst, send, receive, device):
    return pltpu.make_async_remote_copy(
        src_ref=src, dst_ref=dst, send_sem=send, recv_sem=receive, device_id=device,
        device_id_type=MESH,
    )


def project_kernel(
    layer_ref, weight_hbm, *refs,
):
    small_hbm, refs = refs[:10], refs[10:]
    (item_ref, projected_out, columns_ref, rows_ref, table_ref,
     projected_ref, weight_ref, meta_send, bias_ref, sems, load_sems, store_sems), small = (
        refs[:12], refs[12:],
    )
    (segment_ref, mask_ref, position_ref, across_ref, down_ref, query_bias_ref, value_bias_ref,
     text_ref, horiz_ref, vert_ref) = small
    mine = lax.axis_index("seq")
    partner = (1 - mine, lax.axis_index("dp"))
    count, width = layer_ref.shape[1:]
    own = pl.ds(pl.multiple_of(mine * count, LANES), count)
    loads = [
        pltpu.make_async_copy(source, target, load_sems.at[index])
        for index, (source, target) in enumerate(
            list(zip(small_hbm, small))
            + [(layer_ref.at[mine], item_ref.at[own]), (weight_hbm, weight_ref)]
        )
    ]
    for load in loads:
        load.start()
    barrier = pltpu.get_barrier_semaphore()
    pl.semaphore_signal(barrier, inc=1, device_id=partner, device_id_type=MESH)
    pl.semaphore_wait(barrier, 1)
    pieces = count // LANES
    rows_out = [
        remote(
            layer_ref.at[1 - mine, pl.ds(piece * LANES, LANES)],
            item_ref.at[pl.ds(pl.multiple_of(mine * count + piece * LANES, LANES), LANES)],
            sems.at[0, piece], sems.at[1, piece], partner,
        )
        for piece in range(pieces)
    ]
    for copy in rows_out:
        copy.start()
    for load in loads[:-2]:
        load.wait()

    fields = (segment_ref, mask_ref, position_ref, across_ref, down_ref)
    blocks = [
        jnp.concatenate(
            [field[item : item + 1, :] for field in fields] + [jnp.zeros((3, count), jnp.int32)],
            axis=0,
        )
        for item in range(2)
    ]
    meta_send[...] = jnp.where(mine == 0, blocks[1], blocks[0])
    meta_out = remote(
        meta_send, rows_ref.at[:, own], sems.at[0, pieces], sems.at[1, pieces], partner
    )
    meta_out.start()
    rows_ref[:, own] = jnp.where(mine == 0, blocks[0], blocks[1])
    bias_ref[:, :width] = query_bias_ref[...].astype(F32).reshape(1, width)
    bias_ref[:, width : 2 * width] = jnp.zeros((1, width), F32)
    bias_ref[:, 2 * width :] = value_bias_ref[...].astype(F32).reshape(1, width)
    heads, levels = text_ref.shape
    spot = lax.broadcasted_iota(jnp.int32, (levels, LANES), 1)
    level = lax.broadcasted_iota(jnp.int32, (levels, LANES), 0)
    table = jnp.zeros((heads, LANES), F32)
    for source, begin in ((text_ref, 0), (horiz_ref, X_TABLE), (vert_ref, Y_TABLE)):
        table = table + dot_nn(source[...], (spot == level + begin).astype(BF))
    table_ref[...] = jnp.concatenate([table, jnp.zeros((16 - heads, LANES), F32)], axis=0)

    def project(there):
        step = 256

        def body(index, carry):
            columns = pl.ds(pl.multiple_of(index * step, step), step)
            product = dot_nn(item_ref[there], weight_ref[:, columns])
            projected_ref[there, columns] = (product + bias_ref[:, columns]).astype(BF)
            return carry

        lax.fori_loop(0, 3 * width // step, body, 0)

    def stored(index, there):
        return pltpu.make_async_copy(
            projected_ref.at[there], projected_out.at[there], store_sems.at[index]
        )

    for load in loads[-2:]:
        load.wait()
    project(own)
    stored(0, own).start()
    for piece in range(pieces):
        rows_out[piece].wait()
        there = pl.ds(pl.multiple_of((1 - mine) * count + piece * LANES, LANES), LANES)
        project(there)
        stored(1 + piece, there).start()
    meta_out.wait()
    meta = rows_ref[...].astype(F32)
    tall = jnp.concatenate([meta, jnp.zeros((LANES - 8, meta.shape[1]), F32)], axis=0)
    columns_ref[...] = jnp.transpose(tall).astype(jnp.int32)
    stored(0, own).wait()
    for piece in range(pieces):
        there = pl.ds(pl.multiple_of((1 - mine) * count + piece * LANES, LANES), LANES)
        stored(1 + piece, there).wait()


def projected_item(layer_in, fields, qkv_weight, query_bias, value_bias, tables):
    rows = 2 * layer_in.shape[1]
    width = layer_in.shape[2]
    pieces = rows // 2 // LANES
    small = list(fields) + [query_bias, value_bias] + [t.T for t in tables]
    return pl.pallas_call(
        project_kernel,
        in_specs=[HBM] * (2 + len(small)),
        out_specs=[VMEM, HBM, VMEM, VMEM, VMEM],
        out_shape=[
            jax.ShapeDtypeStruct((rows, width), BF),
            jax.ShapeDtypeStruct((rows, 3 * width), BF),
            jax.ShapeDtypeStruct((rows, LANES), jnp.int32),
            jax.ShapeDtypeStruct((8, rows), jnp.int32),
            jax.ShapeDtypeStruct((16, LANES), F32),
        ],
        scratch_shapes=[
            pltpu.VMEM((rows, 3 * width), BF),
            pltpu.VMEM((width, 3 * width), BF),
            pltpu.VMEM((8, rows // 2), jnp.int32),
            pltpu.VMEM((1, 3 * width), F32),
            pltpu.SemaphoreType.DMA((2, pieces + 1)),
            pltpu.SemaphoreType.DMA((len(small) + 2,)),
            pltpu.SemaphoreType.DMA((pieces + 1,)),
        ]
        + [pltpu.VMEM(array.shape, array.dtype) for array in small],
        compiler_params=pltpu.CompilerParams(
            collective_id=1, has_side_effects=True, vmem_limit_bytes=60 * MIB
        ),
        name="projected_item",
    )(layer_in, qkv_weight, *small)


EPSILON = 1e-05
TILE = 256


def vector(ref):
    return ref[...].astype(F32).reshape(1, ref.shape[0])


def gelu_and_slope(x):
    bell = jnp.exp2(-0.7213475204444817 * (x * x))
    rough = 1.0 + 0.23164188826 * jnp.abs(x)
    t = pl.reciprocal(rough, approx=True)
    t = t * (2.0 - rough * t)
    series = t * (
        0.127414796
        + t * (-0.142248368 + t * (0.7107068705 + t * (-0.7265760135 + t * 0.5307027145)))
    )
    tail = bell * series
    below = jnp.where(x >= 0.0, 1.0 - tail, tail)
    return x * below, below + x * (0.3989422804014327 * bell)


def row_mean(block):
    return jnp.mean(block, axis=1, keepdims=True)


def normalized(hidden):
    center = hidden - row_mean(hidden)
    scale = lax.rsqrt(row_mean(center * center) + EPSILON)
    return center * scale, scale


def norm_pulled(grad, unit, scale):
    return scale * (grad - row_mean(grad) - unit * row_mean(grad * unit))


def column_sum(block):
    return jnp.sum(block, axis=0, keepdims=True)


def feed_kernel(
    item_hbm, mixed_hbm, cotangent_ref, out_weight_ref, up_ref, down_ref, *refs,
):
    vectors_hbm, refs = refs[:7], refs[7:]
    (layer_out, total_out, unit_out, scale_out, grad_down_ref, grad_up_ref, small_ref,
     item_ref, mixed_ref, layer_ref, cotangent_all, active, slope, unit, scale_ref, normed, normed_t, total, d_branch, d_branch_t,
     sems, load_sems, tile_sems, store_sems) = refs[:24]
    vectors = refs[24:]
    (out_bias_ref, attn_gain_ref, attn_shift_ref, up_bias_ref, down_bias_ref, ffn_gain_ref,
     ffn_shift_ref) = vectors
    step = pl.program_id(0)
    blocks = pl.num_programs(0) // 2
    rows, width = item_hbm.shape
    count = rows // 2
    mine = lax.axis_index("seq")
    partner = (1 - mine, lax.axis_index("dp"))
    own = pl.ds(pl.multiple_of(mine * count, LANES), count)
    tiles = rows // TILE

    def sent():
        return remote(
            cotangent_ref.at[1 - mine], cotangent_all.at[own], sems.at[0], sems.at[1], partner
        )

    def returned():
        theirs = pl.ds(pl.multiple_of((1 - mine) * count, LANES), count)
        return [
            pltpu.make_async_copy(layer_ref.at[own], layer_out.at[mine], load_sems.at[8]),
            remote(
                layer_ref.at[theirs], layer_out.at[mine], sems.at[2], sems.at[3], partner
            ),
        ]

    def tile_loads(tile):
        there = pl.ds(tile * TILE, TILE)
        return [
            pltpu.make_async_copy(source.at[there], target.at[there], tile_sems.at[index, tile])
            for index, (source, target) in enumerate(
                ((mixed_hbm, mixed_ref), (item_hbm, item_ref))
            )
        ]

    def store(index):
        source, target = (
            (total, total_out), (unit, unit_out), (scale_ref, scale_out),
        )[index]
        return pltpu.make_async_copy(source, target, store_sems.at[index])

    def loads():
        copies = list(zip(vectors_hbm, vectors)) + [(cotangent_ref.at[mine], cotangent_all.at[own])]
        return [
            pltpu.make_async_copy(source, target, load_sems.at[index])
            for index, (source, target) in enumerate(copies)
        ]

    def over_tiles(size, body, carry, unroll=1):
        def run(index, state):
            return body(pl.ds(pl.multiple_of(index * size, size), size), state)

        return lax.fori_loop(0, rows // size, run, carry, unroll=unroll)

    @pl.when(step == 0)
    def _():
        for index in range(rows // TILE):
            for load in tile_loads(index):
                load.start()
        for load in loads():
            load.start()
        barrier = pltpu.get_barrier_semaphore()
        pl.semaphore_signal(barrier, inc=1, device_id=partner, device_id_type=MESH)
        pl.semaphore_wait(barrier, 1)
        sent().start()
        small_ref[...] = jnp.zeros_like(small_ref)
        for load in loads():
            load.wait()
        out_bias, gain, shift = vector(out_bias_ref), vector(attn_gain_ref), vector(attn_shift_ref)

        for index in range(rows // TILE):
            for load in tile_loads(index):
                load.wait()
            there = slice(index * TILE, index * TILE + TILE)
            attn = dot_nn(mixed_ref[there].astype(BF), out_weight_ref[...]) + out_bias
            standard, scale = normalized(item_ref[there].astype(F32) + attn)
            unit[there] = standard
            scale_ref[there] = jnp.broadcast_to(scale, (TILE, LANES))
            result = standard * gain + shift
            normed[there] = result.astype(BF)
            normed_t[:, there] = jnp.transpose(result).astype(BF)
        store(1).start()
        store(2).start()
        total[...] = jnp.zeros_like(total)

    @pl.when(step < blocks)
    def _():
        columns = [slice(begin, begin + TILE) for begin in range(0, width, TILE)]
        low = normed[...]
        following = dot_nn(low, up_ref[:, columns[0]])
        values = []
        for index, here in enumerate(columns):
            product = following
            if index + 1 < len(columns):
                following = dot_nn(low, up_ref[:, columns[index + 1]])
            bias = up_bias_ref[pl.ds(pl.multiple_of(step * width + here.start, LANES), TILE)]
            value, grade = gelu_and_slope(product + bias.astype(F32).reshape(1, TILE))
            values.append(value.astype(BF))
            active[step, :, here] = values[-1]
            slope[step, :, here] = grade.astype(BF)
        values = jnp.concatenate(values, axis=1)
        for here in columns:
            total[:, here] += dot_nn(values, down_ref[:, here])

    @pl.when(step == blocks)
    def _():
        sent().wait()
        gain, shift, bias = vector(ffn_gain_ref), vector(ffn_shift_ref), vector(down_bias_ref)
        first_gain, first_shift = vector(attn_gain_ref), vector(attn_shift_ref)

        def tile(there, sums):
            hidden = unit[there] * first_gain + first_shift + (total[there] + bias)
            standard, scale = normalized(hidden)
            layer_ref[there] = (standard * gain + shift).astype(BF)
            cotangent = cotangent_all[there].astype(F32)
            pulled = norm_pulled(cotangent * gain, standard, scale)
            total[there] = pulled
            low = pulled.astype(BF)
            d_branch[there] = low
            return (
                sums[0] + column_sum(low.astype(F32)),
                sums[1] + column_sum(cotangent * standard),
                sums[2] + column_sum(cotangent),
            )

        zero = jnp.zeros((1, width), F32)
        sums = over_tiles(64, tile, (zero, zero, zero), 4)
        for row, value in zip((5, 6, 7), sums):
            small_ref[row : row + 1] = value

        for copy in returned():
            copy.start()

        def turn(there, carry):
            d_branch_t[:, there] = jnp.transpose(d_branch[there].astype(F32)).astype(BF)
            return carry

        over_tiles(TILE, turn, 0, 3)

    @pl.when(step >= blocks)
    def _():
        block = step - blocks

        columns = [slice(begin, begin + TILE) for begin in range(0, width, TILE)]
        branch = d_branch[...]
        turned = d_branch_t[...]
        following = dot_nt(branch, down_ref[columns[0]])
        values = []
        for index, here in enumerate(columns):
            product = following
            if index + 1 < len(columns):
                following = dot_nt(branch, down_ref[columns[index + 1]])
            grad_down_ref[:, here] = dot_nn(turned, active[block, :, here]).astype(BF)
            d_up = (product * slope[block, :, here].astype(F32)).astype(BF)
            small_ref[pl.ds(8 + block, 1), here] = column_sum(d_up.astype(F32))
            values.append(d_up)
        values = jnp.concatenate(values, axis=1)
        turned = normed_t[...]
        for here in columns:
            grad_up_ref[:, here] = dot_nn(turned, values[:, here]).astype(BF)
            total[:, here] += dot_nt(values, up_ref[here])

    @pl.when(step == 2 * blocks - 1)
    def _():
        store(0).start()
        for copy in returned() + [store(0), store(1), store(2)]:
            copy.wait()


def fed_forward_and_back(
    item, mixed, cotangent, out_weight, up_weight, down_weight, vectors,
):
    rows, width = item.shape
    blocks = up_weight.shape[1] // width
    whole = pl.BlockSpec(memory_space=pltpu.VMEM)
    square = lambda kind: jax.ShapeDtypeStruct((rows, width), kind)
    later = lambda i: jnp.maximum(i - blocks, 0)
    return pl.pallas_call(
        feed_kernel,
        grid=(2 * blocks,),
        in_specs=[HBM, HBM, HBM, whole]
        + [
            pl.BlockSpec((width, width), lambda i: (0, lax.rem(i, blocks))),
            pl.BlockSpec((width, width), lambda i: (lax.rem(i, blocks), 0)),
        ]
        + [HBM] * 7,
        out_specs=[HBM] * 4
        + [
            pl.BlockSpec((width, width), lambda i: (later(i), 0)),
            pl.BlockSpec((width, width), lambda i: (later(i), 0)),
            whole,
        ],
        out_shape=[
            jax.ShapeDtypeStruct((2, rows // 2, width), BF), square(F32), square(F32),
            jax.ShapeDtypeStruct((rows, LANES), F32),
            jax.ShapeDtypeStruct((blocks * width, width), BF),
            jax.ShapeDtypeStruct((blocks * width, width), BF),
            jax.ShapeDtypeStruct((16, width), F32),
        ],
        scratch_shapes=[
            pltpu.VMEM((rows, width), BF),
            pltpu.VMEM((rows, width), F32),
            pltpu.VMEM((rows, width), BF),
            pltpu.VMEM((rows, width), BF),
            pltpu.VMEM((blocks, rows, width), BF),
            pltpu.VMEM((blocks, rows, width), BF),
            pltpu.VMEM((rows, width), F32),
            pltpu.VMEM((rows, LANES), F32),
            pltpu.VMEM((rows, width), BF),
            pltpu.VMEM((width, rows), BF),
            pltpu.VMEM((rows, width), F32),
            pltpu.VMEM((rows, width), BF),
            pltpu.VMEM((width, rows), BF),
            pltpu.SemaphoreType.DMA((4,)),
            pltpu.SemaphoreType.DMA((9,)),
            pltpu.SemaphoreType.DMA((2, rows // TILE)),
            pltpu.SemaphoreType.DMA((3,)),
        ]
        + [pltpu.VMEM(vector.shape, vector.dtype) for vector in vectors],
        compiler_params=pltpu.CompilerParams(
            collective_id=2, has_side_effects=True, vmem_limit_bytes=60 * MIB
        ),
        name="feed_forward",
    )(item, mixed, cotangent, out_weight, up_weight, down_weight, *vectors)


SLOTS = 4


def finish_kernel(
    main_ref, tail_ref, input_hbm, small_ref, diagonal_ref,
    down_ref, up_ref, out_ref, qkv_ref, input_ref, *refs,
):
    singles, (main_in, tail_in, slots, input_in, input_slot, in_sems, out_sems, item_sems) = (
        refs[:12], refs[12:],
    )
    mains, width = main_in.shape[0], main_in.shape[2]
    pairs, across = tail_in.shape[0], tail_in.shape[2]
    hidden = mains // 2
    blocks = mains + pairs

    def load(block):
        if block < mains:
            source, target = main_ref.at[pl.ds(block * width, width)], main_in.at[block]
        else:
            pair = block - mains
            source, target = tail_ref.at[pl.ds(pair * TAIL_ROWS, TAIL_ROWS)], tail_in.at[pair]
        return pltpu.make_async_copy(source, target, in_sems.at[block])

    def stores(block):
        slot, sem = slots.at[block % SLOTS], out_sems.at[block % SLOTS]
        if block < hidden:
            targets = [(slot, down_ref.at[pl.ds(block * width, width)])]
        elif block < mains:
            targets = [(slot, up_ref.at[:, pl.ds((block - hidden) * width, width)])]
        else:
            pair = block - mains
            targets = [
                (
                    slot.at[:, pl.ds(part * LANES, LANES)],
                    qkv_ref.at[:, pl.ds(part * width + pair * LANES, LANES)],
                )
                for part in range(3)
            ]
            down = pl.ds(0, TAIL_ROWS - width)
            targets.append(
                (slot.at[down, pl.ds(across, across)], out_ref.at[out_spot(pair, pairs, width)])
            )
        return [
            pltpu.make_async_copy(source, target, sem.at[index])
            for index, (source, target) in enumerate(targets)
        ]

    load_input = pltpu.make_async_copy(input_hbm, input_in, item_sems.at[0])
    store_input = pltpu.make_async_copy(input_slot, input_ref, item_sems.at[1])
    for block in range(blocks):
        load(block).start()
    load_input.start()
    for block in range(blocks):
        load(block).wait()
        if block >= SLOTS:
            for copy in stores(block - SLOTS):
                copy.wait()
        slot = block % SLOTS
        if block < hidden:
            slots[slot] = jnp.transpose(main_in[block].astype(F32))
        elif block < mains:
            slots[slot] = main_in[block].astype(F32)
        else:
            slots[slot, :, :across] = tail_in[block - mains, :width].astype(F32)
            slots[slot, : TAIL_ROWS - width, across:] = tail_in[block - mains, width:].astype(F32)
        for copy in stores(block):
            copy.start()
    load_input.wait()
    input_slot[...] = input_in[...].astype(F32)
    store_input.start()
    for row in range(8):
        singles[row][...] = small_ref[row]
    for row in range(hidden):
        singles[8][row * width : row * width + width] = small_ref[8 + row]
    heads, levels = singles[9].shape
    diagonals = diagonal_ref[...]
    level = lax.broadcasted_iota(jnp.int32, (LANES, LANES), 1)
    lane = lax.broadcasted_iota(jnp.int32, (LANES, LANES), 0)
    for table, (first, size, skip) in enumerate(((0, 4, 0), (4, 2, 1), (6, 2, 1))):
        total = jnp.zeros((heads, LANES), F32)
        for row in range(size):
            distance = lane + LANES * (row + skip - 2)
            chosen = (bucket(distance) == level).astype(F32)
            total = total + jnp.dot(
                diagonals[:, first + row, :], chosen, preferred_element_type=F32,
                precision=lax.Precision.HIGHEST,
            )
        singles[9 + table][...] = total[:, :levels]
    for block in range(blocks - SLOTS, blocks):
        for copy in stores(block):
            copy.wait()
    store_input.wait()


def finished(main, tail, grad_input, small, diagonals, hidden, levels):
    width = main.shape[1]
    heads = diagonals.shape[0]
    mains = main.shape[0] // width
    pairs = tail.shape[0] // TAIL_ROWS
    single = jax.ShapeDtypeStruct((width,), F32)
    table = jax.ShapeDtypeStruct((heads, levels), F32)
    dma = pltpu.SemaphoreType.DMA
    return pl.pallas_call(
        finish_kernel,
        in_specs=[HBM, HBM, HBM, VMEM, VMEM],
        out_specs=[HBM] * 5 + [VMEM] * 12,
        out_shape=[
            jax.ShapeDtypeStruct((hidden, width), F32),
            jax.ShapeDtypeStruct((width, hidden), F32),
            jax.ShapeDtypeStruct((width, width), F32),
            jax.ShapeDtypeStruct((width, 3 * width), F32),
            jax.ShapeDtypeStruct(grad_input.shape, F32),
        ]
        + [single] * 8
        + [jax.ShapeDtypeStruct((hidden,), F32)]
        + [table] * 3,
        scratch_shapes=[
            pltpu.VMEM((mains, width, width), BF),
            pltpu.VMEM((pairs, TAIL_ROWS, tail.shape[1]), BF),
            pltpu.VMEM((SLOTS, width, width), F32),
            pltpu.VMEM(grad_input.shape, BF),
            pltpu.VMEM(grad_input.shape, F32),
            dma((mains + pairs,)),
            dma((SLOTS, 4)),
            dma((2,)),
        ],
        compiler_params=pltpu.CompilerParams(vmem_limit_bytes=56 * MIB),
        name="finished",
    )(main, tail, grad_input, small, diagonals)


PIECE = 16


class Place:
    def __init__(self, depth):
        place = lax.axis_index("dp")
        self.depth = depth
        self.group = lax.div(place, 4 * depth)
        self.z = lax.rem(lax.div(place, 4), depth)
        self.bits = {
            "x": lax.axis_index("seq"),
            "c": lax.rem(place, 2),
            "y": lax.rem(lax.div(place, 2), 2),
            "a": lax.rem(self.z, 2),
            "b": lax.div(self.z, 2),
        }

    def partner(self, letters):
        bit = {
            letter: 1 - value if letter in letters else value
            for letter, value in self.bits.items()
        }
        z = self.z
        for letter, reach in (("a", 1), ("b", 2)):
            if letter in letters:
                z = z + reach - 2 * reach * self.bits[letter]
        return (bit["x"], (self.group * self.depth + z) * 4 + bit["y"] * 2 + bit["c"])

    def greet(self, met):
        barrier = pltpu.get_barrier_semaphore()
        for letters in met:
            pl.semaphore_signal(
                barrier, inc=1, device_id=self.partner(letters), device_id_type=MESH
            )
        pl.semaphore_wait(barrier, len(met))


def letters_of(depth):
    return "xy" + "ab"[: (depth - 1).bit_length()]


def parsed(routes, depth):
    kept = letters_of(depth)
    parts = []
    for route in routes.split():
        hops = ["".join(letter for letter in hop if letter in kept) for hop in route.split(".")]
        parts.append([hop for hop in hops if hop])
    return parts


def subsets(hop):
    return [
        "".join(letter for index, letter in enumerate(hop) if mask >> index & 1)
        for mask in range(1, 2 ** len(hop))
    ]


class Chunk:
    def __init__(self, place, depth, source, out_ref, offset, spot, scratch):
        _, self.begin, rows, first, columns, _, routes, _ = spot
        self.place, self.source, self.columns = place, source, pl.ds(first, columns)
        self.out_ref, self.out_begin = out_ref, offset + self.begin
        self.parts = parsed(routes, depth)
        self.half = rows // 2
        self.share = self.half // len(self.parts)
        self.hops = max(len(part) for part in self.parts)
        self.work, self.fresh, *landing, self.sends, self.receives, self.locals = scratch
        self.landing = {}
        self.sems = {}
        count = 2
        for part, hops in enumerate(self.parts):
            for hop, letters in enumerate(hops):
                self.landing[part, hop] = landing.pop(0)
                for way in range(2):
                    for index in range(2 ** len(letters) - 1):
                        self.sems[way, part, hop, index] = count
                        count += 1

    def aligned(self, value):
        return pl.multiple_of(value, PIECE)

    def size(self, part, hop):
        return self.share >> sum(len(letters) for letters in self.parts[part][: hop + 1])

    def spot(self, part, hop, other=""):
        start = part * self.share
        for level in range(hop + 1):
            for index, letter in enumerate(self.parts[part][level]):
                bit = self.place.bits[letter]
                if level == hop and letter in other:
                    bit = 1 - bit
                start = start + bit * (self.size(part, level) << index)
        return start

    def out(self, core):
        begin = self.aligned(self.out_begin + core * self.half)
        return self.out_ref.at[pl.ds(begin, self.half), self.columns]

    def held(self, buffer, begin, size):
        return buffer.at[pl.ds(self.aligned(begin), size)]

    def copy(self, index, source, target, letters):
        return remote(
            source, target, self.sends.at[index], self.receives.at[index],
            self.place.partner(letters),
        )

    def pair_down(self):
        core = self.place.bits["c"]
        at = lambda c: self.source.at[
            pl.ds(self.aligned(self.begin + c * self.half), self.half), self.columns
        ]
        return [
            self.copy(0, at(1 - core), self.fresh, "c"),
            pltpu.make_async_copy(at(core), self.work, self.locals.at[0]),
        ]

    def pair_up(self, arriving):
        core = self.place.bits["c"]
        return [
            self.copy(1, self.fresh, self.out(1 - core if arriving else core), "c"),
            pltpu.make_async_copy(self.fresh, self.out(core), self.locals.at[1]),
        ]

    def at_hop(self, hop):
        return [
            (part, hops[hop]) for part, hops in enumerate(self.parts) if hop < len(hops)
        ]

    def down(self, hop):
        copies = []
        for part, letters in self.at_hop(hop):
            size = self.size(part, hop)
            for index, other in enumerate(subsets(letters)):
                copies.append(
                    self.copy(
                        self.sems[0, part, hop, index],
                        self.held(self.work, self.spot(part, hop, other), size),
                        self.landing[part, hop].at[index], other,
                    )
                )
        return copies

    def up(self, hop, arriving):
        copies = []
        for part, letters in self.at_hop(hop):
            mine = self.spot(part, hop)
            size = self.size(part, hop)
            for index, other in enumerate(subsets(letters)):
                target = self.spot(part, hop, other) if arriving else mine
                copies.append(
                    self.copy(
                        self.sems[1, part, hop, index], self.held(self.fresh, mine, size),
                        self.held(self.fresh, target, size), other,
                    )
                )
        return copies

    def add(self, begin, sources, size):
        step = 64 if size % 64 == 0 else 32 if size % 32 == 0 else PIECE

        def body(index, carry):
            offset = self.aligned(index * step)
            there = pl.ds(self.aligned(begin + offset), step)
            total = self.work[there]
            if len(sources) == 1:
                total = total + sources[0][pl.ds(offset, step)]
            else:
                total = total.astype(F32)
                for source in sources:
                    total = total + source[pl.ds(offset, step)].astype(F32)
            self.work[there] = total.astype(BF)
            return carry

        lax.fori_loop(0, size // step, body, 0)

    def stage(self, number):
        hops = self.hops
        ended, started = [], []
        if number == 0:
            started = self.pair_down()
        elif number == 1:
            ended = self.pair_down()
            started = self.down(0)
        elif number <= hops:
            ended = self.down(number - 2)
            started = self.down(number - 1)
        elif number == hops + 1:
            ended = self.down(hops - 1)
            started = self.up(hops - 1, False)
        elif number <= 2 * hops:
            level = 2 * hops + 1 - number
            ended = self.up(level, True)
            started = self.up(level - 1, False)
        elif number == 2 * hops + 1:
            ended = self.up(0, True)
            started = self.pair_up(False)
        else:
            ended = self.pair_up(True)
        for copy in ended:
            copy.wait()
        if number == 1:
            self.add(0, [self.fresh], self.half)
        elif 2 <= number <= hops + 1:
            hop = number - 2
            for part, letters in self.at_hop(hop):
                landing = self.landing[part, hop]
                sources = [landing.at[index] for index in range(2 ** len(letters) - 1)]
                self.add(self.spot(part, hop), sources, self.size(part, hop))
        if number == hops + 1:
            for part, route in enumerate(self.parts):
                last = len(route) - 1
                there = pl.ds(self.aligned(self.spot(part, last)), self.size(part, last))
                self.fresh[there] = self.work[there]
        for copy in started:
            copy.start()


def chunk_scratch(spot, depth):
    _, _, rows, _, columns, _, routes, _ = spot
    parts = parsed(routes, depth)
    landing = []
    copies = 2
    for hops in parts:
        size = rows // 2 // len(parts)
        for letters in hops:
            size >>= len(letters)
            others = 2 ** len(letters) - 1
            copies += 2 * others
            landing.append(pltpu.VMEM((others, size, columns), BF))
    dma = pltpu.SemaphoreType.DMA
    return (
        [pltpu.VMEM((rows // 2, columns), BF)] * 2
        + landing
        + [dma((copies,)), dma((copies,)), dma((2,))]
    )


def loads_of(hop, size):
    if "x" in hop and "y" in hop:
        return [("x", 2 * size), ("y", 2 * size)]
    if hop in ("x", "y"):
        return [(hop, size)]
    if "a" in hop and "b" in hop:
        return [("end", 3 * size), ("middle", 4 * size)]
    return [("end", size), ("middle", 2 * size)] if hop == "b" else [("end", size)]


def planned(chunks, work, depth, hop_count):
    latency, issue, link, pair = 3.5, 0.08, 100e3, 600e3
    free = {}
    now = 3.0
    chains = []
    for rows, columns, need, routes, _ in chunks:
        parts = parsed(routes, depth)
        sizes = [rows // 2 // len(parts)] * len(parts)
        down = []
        for hop in range(max(len(part) for part in parts)):
            loads, copies, added = [], 0, 0
            for index, part in enumerate(parts):
                if hop < len(part):
                    sizes[index] >>= len(part[hop])
                    others = 2 ** len(part[hop]) - 1
                    loads += loads_of(part[hop], sizes[index])
                    copies += others
                    added += sizes[index] * others
            down.append((loads, copies, added, columns))
        first = [([("core", rows // 2)], 1.5, rows // 2, columns)]
        last = [([("core", rows // 2)], 1, 0, columns)]
        chains.append((need, first + down + down[::-1] + last))
    chains.append((len(work), [([("core", 16)], 2, 0, 768)] * hop_count))
    ranks = [chunk[4] for chunk in chunks] + [0]
    position = [0] * len(chains)
    ready = [0.0] * len(chains)
    order = [[] for _ in range(len(work) + 1)]
    done = 0
    while True:
        open_ones = [
            (ranks[i], ready[i], i) for i, (need, chain) in enumerate(chains)
            if position[i] <= len(chain) and need <= done
        ]
        due = [entry for entry in open_ones if entry[1] <= now]
        if not due and done < len(work):
            now += work[done]
            done += 1
            continue
        if not open_ones:
            return order
        _, when, index = min(due) if due else min(open_ones, key=lambda entry: entry[1])
        now = max(now, when)
        chain = chains[index][1]
        stage = position[index]
        order[done].append((index, stage))
        if 0 < stage <= len(chain) // 2:
            now += 1e-6 * chain[stage - 1][2] * chain[stage - 1][3]
        if stage < len(chain):
            loads, copies, _, columns = chain[stage]
            now += issue * copies
            end = now
            for lane, rows in loads:
                rate = pair if lane == "core" else link / 2
                free[lane] = max(now, free.get(lane, 0.0)) + 2 * rows * columns / rate
                end = max(end, free[lane])
            ready[index] = end + latency
        position[index] += 1


def last_kernel(
    depth, plan, orders, counts, *refs,
):
    (meta_ref, rows_ref, projected_hbm, mixed_hbm, log_ref, first_hbm, second_hbm,
     key_image_hbm, bias_hbm, small_ref, gain_ref, item_hbm, weight_hbm, total_hbm, unit_hbm, scale_hbm,
     out_weight_hbm, grad_down_ref, grad_up_ref,
     main_out, tail_out, small_out, diagonal_out, input_out,
     *scratch) = refs
    static, scratch = scratch[:6], scratch[6:]
    (k_ref, v_ref, mixed_ref, grad_ref, first_ref, second_ref, key_image_ref, bias_ref, pair_sems,
     item_ref, weight_ref, d_hidden_ref, unit_ref, scale_ref, load_sems, d_project, item_t, tail, input_grad,
     small_in, diagonal_in, small_sems, item_sems, *scratch) = scratch
    out_weight_ref = item_t
    place = Place(depth)
    step = pl.program_id(0)
    pairs = k_ref.shape[0]
    rows, width = item_hbm.shape
    count = rows // 2
    x = place.bits["x"]
    hidden = grad_down_ref.shape[0]
    sources = ((grad_down_ref, main_out, 0), (grad_up_ref, main_out, hidden), (tail, tail_out, 0))
    chunks = []
    for spot, pieces in zip(plan, counts):
        chunks.append(Chunk(place, depth, *sources[spot[0]], spot, scratch[:pieces]))
        scratch = scratch[pieces:]
    hop_letters = "c" + letters_of(depth)
    wide_hbm = (first_hbm, second_hbm, key_image_hbm, bias_hbm)
    wide_refs = (first_ref, second_ref, key_image_ref, bias_ref)

    def pair_loads(pair):
        copies = []
        held = ((projected_hbm, k_ref, width), (projected_hbm, v_ref, 2 * width))
        for source, target, first in held:
            columns = pl.ds(pl.multiple_of(first + pair * LANES, LANES), LANES)
            copies.append((source.at[:, columns], target.at[pair]))
        heads = pl.ds(2 * pair, 2)
        for source, target in zip(wide_hbm, wide_refs):
            copies.append((source.at[heads], target.at[heads]))
        return [
            pltpu.make_async_copy(source, target, pair_sems.at[pair, index])
            for index, (source, target) in enumerate(copies)
        ]

    def loads(first):
        if first:
            copies = [
                (total_hbm, d_hidden_ref), (unit_hbm, unit_ref), (scale_hbm, scale_ref),
                (out_weight_hbm, out_weight_ref), (item_hbm, item_ref),
            ]
            copies += [
                (mixed_hbm.at[:, pl.ds(pair * LANES, LANES)], mixed_ref.at[pair])
                for pair in range(pairs)
            ]
        else:
            copies = [(weight_hbm, weight_ref)]
        return [
            pltpu.make_async_copy(source, target, load_sems.at[0 if first else 1, index])
            for index, (source, target) in enumerate(copies)
        ]

    def back_to_attention():
        gain = vector(gain_ref)

        def tile(index, sums):
            there = pl.ds(pl.multiple_of(index * 64, 64), 64)
            d_normed = d_hidden_ref[there]
            standard = unit_ref[there]
            d_hidden = norm_pulled(d_normed * gain, standard, scale_ref[there, :1])
            d_hidden_ref[there] = d_hidden
            low = d_hidden.astype(BF)
            input_grad[there] = low
            return (
                sums[0] + column_sum(low.astype(F32)),
                sums[1] + column_sum(d_normed * standard),
                sums[2] + column_sum(d_normed),
            )

        zero = jnp.zeros((1, width), F32)
        sums = lax.fori_loop(0, rows // 64, tile, (zero, zero, zero), unroll=4)
        for row, value in zip((2, 3, 4), sums):
            small_out[row : row + 1] = value
        low = input_grad[...]
        down = TAIL_ROWS - width
        for begin in range(0, width, down):
            first = begin // LANES
            several = range(first, first + down // LANES)
            d_mixed = dot_nt(low, out_weight_ref[begin : begin + down]).astype(BF)
            for index, pair in enumerate(several):
                grad_ref[pair] = d_mixed[:, index * LANES : index * LANES + LANES]
            turned = jnp.concatenate(
                [jnp.transpose(mixed_ref[pair]).astype(BF) for pair in several], axis=0
            )
            for pair in range(pairs):
                rows_of, across = out_spot(pair, pairs, width)
                if rows_of.start == begin:
                    product = dot_nn(turned, low[:, across.start : across.start + across.size])
                    base = pair * TAIL_ROWS + width
                    tail[base : base + down] = product.astype(BF)

    def input_copies():
        return [
            pltpu.make_async_copy(
                input_grad.at[pl.ds(pl.multiple_of(x * count, LANES), count)], input_out.at[x],
                item_sems.at[0],
            ),
            remote(
                input_grad.at[pl.ds(pl.multiple_of((1 - x) * count, LANES), count)],
                input_out.at[x], item_sems.at[1], item_sems.at[2], place.partner("x"),
            ),
        ]

    def small_copies(hop):
        return [
            remote(source, landing.at[hop], small_sems.at[0, kind, hop],
                   small_sems.at[1, kind, hop], place.partner(hop_letters[hop]))
            for kind, (source, landing) in enumerate(
                ((small_out, small_in), (diagonal_out, diagonal_in))
            )
        ]

    def small_stage(hop):
        if hop > 0:
            for copy in small_copies(hop - 1):
                copy.wait()
            small_out[...] = small_out[...] + small_in[hop - 1]
            diagonal_out[...] = diagonal_out[...] + diagonal_in[hop - 1]
        if hop < len(hop_letters):
            for copy in small_copies(hop):
                copy.start()

    def perform(slot):
        for index, stage in orders[slot]:
            if index == len(chunks):
                small_stage(stage)
            else:
                chunks[index].stage(stage)

    @pl.when(step == 0)
    def _():
        for copy in pair_loads(0) + loads(True):
            copy.start()
        met = set(hop_letters)
        for chunk in chunks:
            for hops in chunk.parts:
                for letters in hops:
                    met.update(subsets(letters))
        place.greet(sorted(met))
        small_out[...] = small_ref[...]

    for pair in range(pairs):
        @pl.when(step == pair)
        def _(pair=pair):
            perform(pair)

    @pl.when(step == 0)
    def _():
        for pair in range(1, pairs):
            for copy in pair_loads(pair):
                copy.start()
        for copy in loads(False):
            copy.start()
        static_prepare(meta_ref, static)
        for copy in loads(True):
            copy.wait()
        back_to_attention()
        for tile in range(rows // TILE):
            there = slice(tile * TILE, tile * TILE + TILE)
            item_t[:, there] = jnp.transpose(item_ref[there].astype(F32)).astype(BF)

    for copy in pair_loads(step):
        copy.wait()
    (dq_even, dk_even, dv_even), (dq_odd, dk_odd, dv_odd) = [
        head_back(
            parity, step, rows_ref, wide_refs, k_ref, v_ref, mixed_ref, grad_ref, log_ref,
            static, diagonal_out,
        )
        for parity in range(2)
    ]
    even = own_lanes(0, rows)
    pieces = [
        jnp.transpose(jnp.concatenate([dq_even, dq_odd], axis=0)).astype(BF),
        jnp.where(even, dk_even, dk_odd).astype(BF),
        jnp.where(even, dv_even, dv_odd).astype(BF),
    ]
    for part, piece in enumerate(pieces):
        d_project[:, pl.ds(pl.multiple_of(part * width + step * LANES, LANES), LANES)] = piece
    slab = pl.ds(pl.multiple_of(step * TAIL_ROWS, TAIL_ROWS), width)
    tail[slab] = dot_nn(item_t[...], jnp.concatenate(pieces, axis=1)).astype(BF)

    @pl.when(step == 0)
    def _():
        for copy in loads(False):
            copy.wait()

    @pl.when(step == pairs - 1)
    def _():
        perform(pairs)
        for begin in range(0, width, TILE):
            here = slice(begin, begin + TILE)
            total = d_hidden_ref[:, here] + dot_nt(d_project[...], weight_ref[here])
            input_grad[:, here] = total.astype(BF)
        for copy in input_copies():
            copy.start()
        for begin in range(0, width, TILE):
            here = slice(begin, begin + TILE)
            there = slice(2 * width + begin, 2 * width + begin + TILE)
            small_out[0:1, here] = column_sum(d_project[:, here].astype(F32))
            small_out[1:2, here] = column_sum(d_project[:, there].astype(F32))
        perform(pairs + 1)
        for copy in input_copies():
            copy.wait()


TAIL_ROWS = 1024


def out_spot(pair, pairs, width):
    down = TAIL_ROWS - width
    across = width * width // (pairs * down)
    per_row = width // across
    return (
        pl.ds(pair // per_row * down, down),
        pl.ds(pair % per_row * across, across),
    )


def summed_with_attention_back(
    meta_columns, meta_rows, projected, mixed, logs, wide_arrays, item, qkv_weight,
    total, unit, scale, out_weight, attn_gain, small, grad_down, grad_up,
):
    size = lax.axis_size("dp")
    depth = 4 if size % 16 == 0 else size // 4
    rows, width = item.shape
    pairs = width // LANES
    hidden = grad_down.shape[0]
    hops = len(letters_of(depth)) + 1
    work = [6.8] * pairs + [4.0]
    tall, wide, slim = 1024, 3 * LANES, 2 * LANES
    plan = [
        (0, 0, 2 * tall, 0, width, 0, "a.b.x.y x.y.a.b", 1),
        (0, 2 * tall, tall, 0, width, 0, "x.a.y.b y.a.b.x", 2),
        (1, 0, 3 * tall, 0, slim, 0, "a.b.x.y y.x.a.b", 4),
        (1, 0, 3 * tall, slim, slim, 0, "y.a.x.b x.y.a.b", 0),
        (1, 0, 3 * tall, 2 * slim, slim, 0, "x.y.a.b y.x.a.b", 2),
        (2, 0, tall, 0, wide, 1, "y.x.a.b a.b.x.y", 3),
        (2, tall, tall, 0, wide, 2, "xy.a.b", 2),
        (2, 2 * tall, tall, 0, wide, 3, "x.y.ab y.ab.x", 3),
        (2, 3 * tall, tall, 0, wide, 4, "xy.a.b", 1),
        (2, 4 * tall, tall, 0, wide, 5, "xy.a.b", 1),
        (2, 5 * tall, tall, 0, wide, 6, "ab.y.x y.ab.x", 2),
    ]
    orders = planned([(spot[2],) + spot[4:] for spot in plan], work, depth, hops)

    whole = pl.BlockSpec(memory_space=pltpu.VMEM)
    diagonals = jax.ShapeDtypeStruct((2 * pairs, 8, LANES), F32)
    dma = pltpu.SemaphoreType.DMA
    scratch = []
    for spot in plan:
        scratch.append(chunk_scratch(spot, depth))
    main, tail, small, diagonals, grad_input = pl.pallas_call(
        functools.partial(last_kernel, depth, plan, orders, [len(pieces) for pieces in scratch]),
        grid=(pairs,),
        in_specs=[whole] * 2 + [HBM] * 2 + [whole] + [HBM] * 4 + [whole] * 2 + [HBM] * 8,
        out_specs=[HBM, HBM, whole, whole, HBM],
        out_shape=[
            jax.ShapeDtypeStruct((2 * hidden, width), BF),
            jax.ShapeDtypeStruct((pairs * TAIL_ROWS, 3 * LANES), BF),
            jax.ShapeDtypeStruct(small.shape, F32),
            diagonals,
            jax.ShapeDtypeStruct((2, rows // 2, width), BF),
        ],
        scratch_shapes=[pltpu.VMEM((rows, LANES), BF)] * 3
        + [pltpu.VMEM((LANES, rows), BF)] * 3
        + [pltpu.VMEM((pairs, rows, LANES), kind) for kind in (BF, BF, F32, BF)]
        + [pltpu.VMEM(array.shape, BF) for array in wide_arrays]
        + [
            dma((pairs, 6)),
            pltpu.VMEM((rows, width), BF),
            pltpu.VMEM((width, 3 * width), BF),
            pltpu.VMEM((rows, width), F32),
            pltpu.VMEM((rows, width), F32),
            pltpu.VMEM((rows, LANES), F32),
            dma((2, 5 + pairs)),
            pltpu.VMEM((rows, 3 * width), BF),
            pltpu.VMEM((width, rows), BF),
            pltpu.VMEM((pairs * TAIL_ROWS, 3 * LANES), BF),
            pltpu.VMEM((rows, width), BF),
            pltpu.VMEM((hops,) + small.shape, F32),
            pltpu.VMEM((hops,) + diagonals.shape, F32),
            dma((2, 2, hops)),
            dma((3,)),
        ]
        + [piece for pieces in scratch for piece in pieces],
        compiler_params=pltpu.CompilerParams(
            collective_id=0, has_side_effects=True, vmem_limit_bytes=62 * MIB
        ),
        name="summed_with_attention_back",
    )(meta_columns, meta_rows, projected, mixed, logs, *wide_arrays,
      small, attn_gain, item, qkv_weight, total, unit, scale, out_weight, grad_down, grad_up)
    span = 4 * depth
    if size > span:
        groups = [list(range(first, size, span)) for first in range(span)]
        main, tail, small, diagonals = lax.psum(
            (main.astype(F32), tail.astype(F32), small, diagonals), "dp",
            axis_index_groups=groups,
        )
        main, tail = main.astype(BF), tail.astype(BF)
    return main, tail, small, diagonals, grad_input


def per_device(
    layer_in, segment, key_mask, position, layout_x, layout_y,
    qkv_weight, query_bias, value_bias, out_weight, out_bias, attn_gain, attn_shift,
    up_weight, up_bias, down_weight, down_bias, ffn_gain, ffn_shift,
    text_table, horiz_table, vert_table, cotangent,
):
    width = layer_in.shape[-1]
    item, projected, meta_columns, meta_rows, table_rows = projected_item(
        layer_in, (segment, key_mask, position, layout_x, layout_y),
        qkv_weight, query_bias, value_bias, (text_table, horiz_table, vert_table),
    )
    mixed, logs, *wide_arrays = attention_forward(meta_columns, meta_rows, table_rows, projected, width)
    layer_out, total, unit, scale, grad_down, grad_up, small = fed_forward_and_back(
        item, mixed, cotangent, out_weight, up_weight, down_weight,
        (out_bias, attn_gain, attn_shift, up_bias, down_bias, ffn_gain, ffn_shift),
    )
    main, tail, small, diagonals, grad_input = summed_with_attention_back(
        meta_columns, meta_rows, projected, mixed, logs, wide_arrays, item, qkv_weight,
        total, unit, scale, out_weight, attn_gain, small, grad_down, grad_up,
    )
    done = finished(
        main, tail, grad_input, small, diagonals, up_weight.shape[1], text_table.shape[0]
    )
    sum_down, sum_up, sum_out, sum_qkv, grad_input = done[:5]
    singles, tables = done[5:14], [t.T for t in done[14:]]
    return (
        layer_out, grad_input, sum_qkv, singles[0], singles[1], sum_out, singles[2], singles[3],
        singles[4], sum_up, singles[8], sum_down, singles[5], singles[6], singles[7],
        tables[0], tables[1], tables[2],
    )


def solution(mesh):
    rows = P("dp", "seq", None)
    marks_spec = P("dp", "seq")
    return jax.shard_map(
        per_device,
        mesh=mesh,
        in_specs=(rows,) + (marks_spec,) * 5 + (P(),) * 16 + (rows,),
        out_specs=(rows, rows) + (P(),) * 16,
        check_vma=False,
    )
```

profile of v0, /device:TPU:0, one launch (start us, length us, event | category | flops | bytes accessed | tf_op | source)
XLA Modules:
  0.0 246.4 jit_solution(7632235118304295252)
XLA Ops:
  0.7 20.9 %projected_item.1 = (bf16[768,768]{1,0:T(8,128)(2,1)}, bf16[768,2304]{1,0:T(8,128)(2,1)}, s32[768,128]{1,0:T(8,128)}, s32[8,768]{1,0:T(8,128)}, f32[16,128]{1,0:T(8,128)}) custom-call(bf16[2,384,768]{2,1,0:T(8,128)(2,1)} %layer_ref.1, bf16[768,2304]{1,0:T(8,128)(2,1)} %refs_12_.1, s32[2,384]{1,0:T(2,128)} %refs_0_.2, s32[2,384]{1,0:T(2,128)} %refs_1_.2, ...), custom_call_target="tpu_custom_call" | custom-call | tf_op jit(solution)/shard_map/projected_item/pallas_call | solution.py:551
  21.6 19.2 %attention_forward.1 = (f32[768,768]{1,0:T(8,128)}, f32[6,2,768]{2,1,0:T(2,128)}, bf16[12,768,128]{2,1,0:T(8,128)(2,1)}, bf16[12,768,128]{2,1,0:T(8,128)(2,1)}, ...) custom-call(s32[768,128]{1,0:T(8,128)} %get-tuple-element.59.meta_ref.refs_0_, ...), custom_call_target="tpu_custom_call" | custom-call | tf_op jit(solution)/shard_map/attention_forward/pallas_call | solution.py:260
  40.8 45.8 %feed_forward.1 = (bf16[2,384,768]{2,1,0:T(8,128)(2,1)}, f32[768,768]{1,0:T(8,128)}, f32[768,768]{1,0:T(8,128)}, f32[768,128]{1,0:T(8,128)}, bf16[3072,768]{1,0:...) custom-call(bf16[768,768]{1,0:T(8,128)(2,1)} %get-tuple-element.58.item_hbm.refs_11_, ...), custom_call_target="tpu_custom_call" | custom-call | tf_op jit(solution)/shard_map/feed_forward/pallas_call | solution.py:803
  86.7 142.4 %summed_with_attention_back.1 = (bf16[6144,768]{1,0:T(8,128)(2,1)}, bf16[6144,384]{1,0:T(8,128)(2,1)}, f32[16,768]{1,0:T(8,128)}, f32[12,8,128]{2,1,0:T(8,128)}, bf16[2,384,768]{2,1,0:T(8,128)(2,1)}) custom-call(s32[768,128]{1,0:T(8,128)} %get-tuple-element.59.meta_ref.refs_0_, s32[8,768]{1,0:T(8,128)} %get-tuple-element.60.rows_ref.refs_1_, ...), custom_call_target="tpu_custom_call" | custom-call | tf_op jit(solution)/shard_map/summed_with_attention_back/pallas_call | solution.py:1549
  229.1 0.0 copy-start
  229.1 16.3 %finished.1 = (f32[3072,768]{1,0:T(8,128)}, f32[768,3072]{1,0:T(8,128)}, f32[768,768]{1,0:T(8,128)}, f32[768,2304]{1,0:T(8,128)}, f32[2,384,768]{2,1,0:T(8,128)}...) custom-call(bf16[6144,768]{1,0:T(8,128)(2,1)} %get-tuple-element.76., ...), custom_call_target="tpu_custom_call" | custom-call | tf_op jit(solution)/shard_map/finished/pallas_call | solution.py:954
  245.4 0.0 copy-done
  245.4 1.0 copy.42
Async XLA Ops:
  229.1 16.3 %copy-start = (bf16[2,384,768]{2,1,0:T(8,128)(2,1)S(1)}, bf16[2,384,768]{2,1,0:T(8,128)(2,1)}, u32[]{:S(2)}) copy-start(bf16[2,384,768]{2,1,0:T(8,128)(2,1)} %get-tuple-element.116) | copy-start | bytes 3538948
where the time goes:
time: 247 us; the launch traced here: 246 us
  Pallas kernels  245 us (99%)
    pallas_call x1, Pallas kernels, summed_with_attention_back(): pl.pallas_call(functools.partial(last_kernel, depth, plan, orders, [len(p...  142 us
    pallas_call x1, Pallas kernels, fed_forward_and_back(): pl.pallas_call(feed_kernel, grid=(2 * blocks,), in_specs=[HBM, HBM, HBM,...  45.8 us
    pallas_call x1, Pallas kernels, projected_item(): pl.pallas_call(project_kernel, in_specs=[HBM] * (2 + len(small)), out_spe...  20.9 us
    pallas_call x1, Pallas kernels, attention_forward(): pl.pallas_call(forward_kernel, grid=(pairs,), in_specs=[whole(meta_column...  19.2 us
    pallas_call x1, Pallas kernels, finished(): pl.pallas_call(finish_kernel, in_specs=[HBM, HBM, HBM, VMEM, VMEM], out_s...  16.3 us

commit v1 on v0

--- a/solution.py
+++ b/solution.py
@@ -1368,6 +1368,8 @@
         sums = lax.fori_loop(0, rows // 64, tile, (zero, zero, zero), unroll=4)
         for row, value in zip((2, 3, 4), sums):
             small_out[row : row + 1] = value
+
+    def back_to_heads():
         low = input_grad[...]
         down = TAIL_ROWS - width
         for begin in range(0, width, down):
@@ -1436,13 +1438,9 @@
         place.greet(sorted(met))
         small_out[...] = small_ref[...]
 
-    for pair in range(pairs):
-        @pl.when(step == pair)
-        def _(pair=pair):
-            perform(pair)
-
     @pl.when(step == 0)
     def _():
+        perform(0)
         for pair in range(1, pairs):
             for copy in pair_loads(pair):
                 copy.start()
@@ -1452,9 +1450,16 @@
         for copy in loads(True):
             copy.wait()
         back_to_attention()
+        perform(1)
+        back_to_heads()
         for tile in range(rows // TILE):
             there = slice(tile * TILE, tile * TILE + TILE)
             item_t[:, there] = jnp.transpose(item_ref[there].astype(F32)).astype(BF)
+
+    for pair in range(pairs):
+        @pl.when(step == pair)
+        def _(pair=pair):
+            perform(2 + pair)
 
     for copy in pair_loads(step):
         copy.wait()
@@ -1483,7 +1488,7 @@
 
     @pl.when(step == pairs - 1)
     def _():
-        perform(pairs)
+        perform(pairs + 2)
         for begin in range(0, width, TILE):
             here = slice(begin, begin + TILE)
             total = d_hidden_ref[:, here] + dot_nt(d_project[...], weight_ref[here])
@@ -1495,7 +1500,7 @@
             there = slice(2 * width + begin, 2 * width + begin + TILE)
             small_out[0:1, here] = column_sum(d_project[:, here].astype(F32))
             small_out[1:2, here] = column_sum(d_project[:, there].astype(F32))
-        perform(pairs + 1)
+        perform(pairs + 3)
         for copy in input_copies():
             copy.wait()
 
@@ -1523,7 +1528,7 @@
     pairs = width // LANES
     hidden = grad_down.shape[0]
     hops = len(letters_of(depth)) + 1
-    work = [6.8] * pairs + [4.0]
+    work = [5.0, 4.0] + [6.5] * pairs + [4.0]
     tall, wide, slim = 1024, 3 * LANES, 2 * LANES
     plan = [
         (0, 0, 2 * tall, 0, width, 0, "a.b.x.y x.y.a.b", 1),
@@ -1531,12 +1536,12 @@
         (1, 0, 3 * tall, 0, slim, 0, "a.b.x.y y.x.a.b", 4),
         (1, 0, 3 * tall, slim, slim, 0, "y.a.x.b x.y.a.b", 0),
         (1, 0, 3 * tall, 2 * slim, slim, 0, "x.y.a.b y.x.a.b", 2),
-        (2, 0, tall, 0, wide, 1, "y.x.a.b a.b.x.y", 3),
-        (2, tall, tall, 0, wide, 2, "xy.a.b", 2),
-        (2, 2 * tall, tall, 0, wide, 3, "x.y.ab y.ab.x", 3),
-        (2, 3 * tall, tall, 0, wide, 4, "xy.a.b", 1),
-        (2, 4 * tall, tall, 0, wide, 5, "xy.a.b", 1),
-        (2, 5 * tall, tall, 0, wide, 6, "ab.y.x y.ab.x", 2),
+        (2, 0, tall, 0, wide, 3, "y.x.a.b a.b.x.y", 3),
+        (2, tall, tall, 0, wide, 4, "xy.a.b", 2),
+        (2, 2 * tall, tall, 0, wide, 5, "x.y.ab y.ab.x", 3),
+        (2, 3 * tall, tall, 0, wide, 6, "xy.a.b", 1),
+        (2, 4 * tall, tall, 0, wide, 7, "xy.a.b", 1),
+        (2, 5 * tall, tall, 0, wide, 8, "ab.y.x y.ab.x", 2),
     ]
     orders = planned([(spot[2],) + spot[4:] for spot in plan], work, depth, hops)
 

time: 247 us -> 249 us (level)
  no operation moved by 1% of the time
where the time goes in v1:
time: 249 us
  Pallas kernels  247 us (99%)
    pallas_call x1, Pallas kernels, summed_with_attention_back(): pl.pallas_call(functools.partial(last_kernel, depth, plan, orders, [len(p...  145 us
    pallas_call x1, Pallas kernels, fed_forward_and_back(): pl.pallas_call(feed_kernel, grid=(2 * blocks,), in_specs=[HBM, HBM, HBM,...  45.8 us
    pallas_call x1, Pallas kernels, projected_item(): pl.pallas_call(project_kernel, in_specs=[HBM] * (2 + len(small)), out_spe...  20.9 us
    pallas_call x1, Pallas kernels, attention_forward(): pl.pallas_call(forward_kernel, grid=(pairs,), in_specs=[whole(meta_column...  19.2 us
    pallas_call x1, Pallas kernels, finished(): pl.pallas_call(finish_kernel, in_specs=[HBM, HBM, HBM, VMEM, VMEM], out_s...  16.3 us

profile of v1, /device:TPU:0, one launch (start us, length us, event | category | flops | bytes accessed | tf_op | source)
XLA Modules:
  0.0 248.8 jit_solution(5881590532143003884)
XLA Ops:
  0.7 20.9 %projected_item.1 = (bf16[768,768]{1,0:T(8,128)(2,1)}, bf16[768,2304]{1,0:T(8,128)(2,1)}, s32[768,128]{1,0:T(8,128)}, s32[8,768]{1,0:T(8,128)}, f32[16,128]{1,0:T(8,128)}) custom-call(bf16[2,384,768]{2,1,0:T(8,128)(2,1)} %layer_ref.1, bf16[768,2304]{1,0:T(8,128)(2,1)} %refs_12_.1, s32[2,384]{1,0:T(2,128)} %refs_0_.2, s32[2,384]{1,0:T(2,128)} %refs_1_.2, ...), custom_call_target="tpu_custom_call" | custom-call | tf_op jit(solution)/shard_map/projected_item/pallas_call | solution.py:551
  21.6 19.2 %attention_forward.1 = (f32[768,768]{1,0:T(8,128)}, f32[6,2,768]{2,1,0:T(2,128)}, bf16[12,768,128]{2,1,0:T(8,128)(2,1)}, bf16[12,768,128]{2,1,0:T(8,128)(2,1)}, ...) custom-call(s32[768,128]{1,0:T(8,128)} %get-tuple-element.59.meta_ref.refs_0_, ...), custom_call_target="tpu_custom_call" | custom-call | tf_op jit(solution)/shard_map/attention_forward/pallas_call | solution.py:260
  40.8 45.8 %feed_forward.1 = (bf16[2,384,768]{2,1,0:T(8,128)(2,1)}, f32[768,768]{1,0:T(8,128)}, f32[768,768]{1,0:T(8,128)}, f32[768,128]{1,0:T(8,128)}, bf16[3072,768]{1,0:...) custom-call(bf16[768,768]{1,0:T(8,128)(2,1)} %get-tuple-element.58.item_hbm.refs_11_, ...), custom_call_target="tpu_custom_call" | custom-call | tf_op jit(solution)/shard_map/feed_forward/pallas_call | solution.py:803
  86.7 144.9 %summed_with_attention_back.1 = (bf16[6144,768]{1,0:T(8,128)(2,1)}, bf16[6144,384]{1,0:T(8,128)(2,1)}, f32[16,768]{1,0:T(8,128)}, f32[12,8,128]{2,1,0:T(8,128)}, bf16[2,384,768]{2,1,0:T(8,128)(2,1)}) custom-call(s32[768,128]{1,0:T(8,128)} %get-tuple-element.59.meta_ref.refs_0_, s32[8,768]{1,0:T(8,128)} %get-tuple-element.60.rows_ref.refs_1_, ...), custom_call_target="tpu_custom_call" | custom-call | tf_op jit(solution)/shard_map/summed_with_attention_back/pallas_call | solution.py:1554
  231.5 0.0 copy-start
  231.5 16.3 %finished.1 = (f32[3072,768]{1,0:T(8,128)}, f32[768,3072]{1,0:T(8,128)}, f32[768,768]{1,0:T(8,128)}, f32[768,2304]{1,0:T(8,128)}, f32[2,384,768]{2,1,0:T(8,128)}...) custom-call(bf16[6144,768]{1,0:T(8,128)(2,1)} %get-tuple-element.76., ...), custom_call_target="tpu_custom_call" | custom-call | tf_op jit(solution)/shard_map/finished/pallas_call | solution.py:954
  247.8 0.0 copy-done
  247.8 1.0 copy.42
Async XLA Ops:
  231.5 16.3 %copy-start = (bf16[2,384,768]{2,1,0:T(8,128)(2,1)S(1)}, bf16[2,384,768]{2,1,0:T(8,128)(2,1)}, u32[]{:S(2)}) copy-start(bf16[2,384,768]{2,1,0:T(8,128)(2,1)} %get-tuple-element.116) | copy-start | bytes 3538948

commit v2 on v0

--- a/solution.py
+++ b/solution.py
@@ -1426,7 +1426,12 @@
 
     @pl.when(step == 0)
     def _():
-        for copy in pair_loads(0) + loads(True):
+        for copy in loads(True):
+            copy.start()
+        for pair in range(pairs):
+            for copy in pair_loads(pair):
+                copy.start()
+        for copy in loads(False):
             copy.start()
         met = set(hop_letters)
         for chunk in chunks:
@@ -1443,11 +1448,6 @@
 
     @pl.when(step == 0)
     def _():
-        for pair in range(1, pairs):
-            for copy in pair_loads(pair):
-                copy.start()
-        for copy in loads(False):
-            copy.start()
         static_prepare(meta_ref, static)
         for copy in loads(True):
             copy.wait()

time: 247 us -> 249 us (level)
    pallas_call x1, Pallas kernels: 142 us -> 145 us  [summed_with_attention_back(): pl.pallas_call(functools.partial(last_kernel, depth, plan, orders, [len(p...]
where the time goes in v2:
time: 249 us
  Pallas kernels  247 us (99%)
    pallas_call x1, Pallas kernels, summed_with_attention_back(): pl.pallas_call(functools.partial(last_kernel, depth, plan, orders, [len(p...  145 us
    pallas_call x1, Pallas kernels, fed_forward_and_back(): pl.pallas_call(feed_kernel, grid=(2 * blocks,), in_specs=[HBM, HBM, HBM,...  45.8 us
    pallas_call x1, Pallas kernels, projected_item(): pl.pallas_call(project_kernel, in_specs=[HBM] * (2 + len(small)), out_spe...  20.9 us
    pallas_call x1, Pallas kernels, attention_forward(): pl.pallas_call(forward_kernel, grid=(pairs,), in_specs=[whole(meta_column...  19.2 us
    pallas_call x1, Pallas kernels, finished(): pl.pallas_call(finish_kernel, in_specs=[HBM, HBM, HBM, VMEM, VMEM], out_s...  16.3 us

profile of v2, /device:TPU:0, one launch (start us, length us, event | category | flops | bytes accessed | tf_op | source)
XLA Modules:
  0.0 249.2 jit_solution(377535261568780020)
XLA Ops:
  0.7 20.9 %projected_item.1 = (bf16[768,768]{1,0:T(8,128)(2,1)}, bf16[768,2304]{1,0:T(8,128)(2,1)}, s32[768,128]{1,0:T(8,128)}, s32[8,768]{1,0:T(8,128)}, f32[16,128]{1,0:T(8,128)}) custom-call(bf16[2,384,768]{2,1,0:T(8,128)(2,1)} %layer_ref.1, bf16[768,2304]{1,0:T(8,128)(2,1)} %refs_12_.1, s32[2,384]{1,0:T(2,128)} %refs_0_.2, s32[2,384]{1,0:T(2,128)} %refs_1_.2, ...), custom_call_target="tpu_custom_call" | custom-call | tf_op jit(solution)/shard_map/projected_item/pallas_call | solution.py:551
  21.6 19.2 %attention_forward.1 = (f32[768,768]{1,0:T(8,128)}, f32[6,2,768]{2,1,0:T(2,128)}, bf16[12,768,128]{2,1,0:T(8,128)(2,1)}, bf16[12,768,128]{2,1,0:T(8,128)(2,1)}, ...) custom-call(s32[768,128]{1,0:T(8,128)} %get-tuple-element.59.meta_ref.refs_0_, ...), custom_call_target="tpu_custom_call" | custom-call | tf_op jit(solution)/shard_map/attention_forward/pallas_call | solution.py:260
  40.8 45.8 %feed_forward.1 = (bf16[2,384,768]{2,1,0:T(8,128)(2,1)}, f32[768,768]{1,0:T(8,128)}, f32[768,768]{1,0:T(8,128)}, f32[768,128]{1,0:T(8,128)}, bf16[3072,768]{1,0:...) custom-call(bf16[768,768]{1,0:T(8,128)(2,1)} %get-tuple-element.58.item_hbm.refs_11_, ...), custom_call_target="tpu_custom_call" | custom-call | tf_op jit(solution)/shard_map/feed_forward/pallas_call | solution.py:803
  86.7 145.2 %summed_with_attention_back.1 = (bf16[6144,768]{1,0:T(8,128)(2,1)}, bf16[6144,384]{1,0:T(8,128)(2,1)}, f32[16,768]{1,0:T(8,128)}, f32[12,8,128]{2,1,0:T(8,128)}, bf16[2,384,768]{2,1,0:T(8,128)(2,1)}) custom-call(s32[768,128]{1,0:T(8,128)} %get-tuple-element.59.meta_ref.refs_0_, s32[8,768]{1,0:T(8,128)} %get-tuple-element.60.rows_ref.refs_1_, ...), custom_call_target="tpu_custom_call" | custom-call | tf_op jit(solution)/shard_map/summed_with_attention_back/pallas_call | solution.py:1549
  231.9 0.0 copy-start
  231.9 16.3 %finished.1 = (f32[3072,768]{1,0:T(8,128)}, f32[768,3072]{1,0:T(8,128)}, f32[768,768]{1,0:T(8,128)}, f32[768,2304]{1,0:T(8,128)}, f32[2,384,768]{2,1,0:T(8,128)}...) custom-call(bf16[6144,768]{1,0:T(8,128)(2,1)} %get-tuple-element.76., ...), custom_call_target="tpu_custom_call" | custom-call | tf_op jit(solution)/shard_map/finished/pallas_call | solution.py:954
  248.2 0.0 copy-done
  248.2 1.0 copy.42
Async XLA Ops:
  231.9 16.3 %copy-start = (bf16[2,384,768]{2,1,0:T(8,128)(2,1)S(1)}, bf16[2,384,768]{2,1,0:T(8,128)(2,1)}, u32[]{:S(2)}) copy-start(bf16[2,384,768]{2,1,0:T(8,128)(2,1)} %get-tuple-element.116) | copy-start | bytes 3538948
